TPU v7x, 32 devices: a whole 2x2x4 slice. The times are simulated.
32 devices in a mesh: groups: 2 (over y), rows: 8 (over z, x), blocks: 2 (over core).
Axes of the slice: x: 2, y: 2, z: 4, core: 2. Of those that a mesh axis runs over, the one named last changes fastest.
Arguments:
- adjoint_in: bfloat16 [16, 16, 256], P(('groups', 'rows')), parts along dimension 0, may hold values from -6 to 6
- far_u: bfloat16 [16, 2, 128, 32, 256], P(('groups', 'rows'), 'blocks'), parts along dimension 0, may hold values from -0.375 to 0.375
- far_v: bfloat16 [16, 2, 128, 32, 256], P(('groups', 'rows'), 'blocks'), parts along dimension 0, may hold values from -0.09375 to 0.09375
- far_cols: int32 [16, 2, 128], P(('groups', 'rows'), 'blocks'), parts along dimension 0, may hold values from 0 to 7, as said below
- far_counts: int32 [16, 2], P(('groups', 'rows'), 'blocks'), parts along dimension 0, may hold values from 96 to 128, as said below
- near_blocks: bfloat16 [16, 2, 4, 256, 256], P(('groups', 'rows'), 'blocks'), parts along dimension 0, may hold values from -0.125 to 0.125
- near_cols: int32 [16, 2, 4], P(('groups', 'rows'), 'blocks'), parts along dimension 0, may hold values from 0 to 7, as said below
Outputs:
- adjoint_out: float32 [16, 16, 256], P(('groups', 'rows'), 'blocks'), parts along dimension 0
There are 2 independent parts, one for each index of `groups`. A program takes and returns all parts, laid end to end along the dimension named above; each array names one. Nothing has to cross between parts.
Inputs may be any that keep to these rules, and one draw needn't show every extreme that they name: `far_cols`: among the first far_counts[r, b] slots of one (r, b), no column cluster is named more than 16 times; in every draw one column cluster is named by the first 16 slots of every (r, b). `far_counts`: some (r, b) has exactly 128 live slots. near_cols[r, b, j] differs from r by at most one.
All inputs are finite; a program needn't handle non-finite values.
Results may differ from a plain program's by a relative error of at most 0.0023.
Values may be sent and summed in bfloat16 or wider, within the bound.
A program may use at most 64 MiB of HBM per device.

v0:
```python
import jax
import jax.numpy as jnp
from jax import lax
from jax.sharding import PartitionSpec as P


def passed_along(x, axis, by):
    devices = lax.axis_size(axis)
    pairs = [(i, i + by) for i in range(devices) if 0 <= i + by < devices]
    return lax.ppermute(x, axis, pairs)


def slot_places(targets, live_slots, capacity, row_count):
    slot_ids = jnp.arange(targets.shape[0], dtype=jnp.int32)
    same = (
        (targets[:, None] == targets[None, :])
        & live_slots[None, :]
        & (slot_ids[None, :] < slot_ids[:, None])
    )
    slot_rank = jnp.sum(same.astype(jnp.int32), axis=1)
    return jnp.where(live_slots, targets * capacity + slot_rank, row_count * capacity)


def masked_products(coefficients, v_blocks, live_slots):
    products = jnp.einsum(
        "fik,fkl->fil", coefficients, v_blocks, preferred_element_type=jnp.float32
    )
    return jnp.where(live_slots[:, None, None], products, 0.0)


def on_device(adjoint_in, far_u, far_v, far_cols, far_counts, near_blocks, near_cols):
    vector_row = adjoint_in[0]
    u_blocks = far_u[0, 0]
    v_blocks = far_v[0, 0]
    targets = far_cols[0, 0]
    live_count = far_counts[0, 0]
    near_row = near_blocks[0, 0]
    near_targets = near_cols[0, 0]
    row_count = lax.axis_size("rows")
    position = lax.axis_index("rows")
    far_total = u_blocks.shape[0]
    rhs_count = vector_row.shape[0]
    width = vector_row.shape[1]
    capacity = max(2, (far_total + row_count - 1) // row_count)
    live_slots = jnp.arange(far_total, dtype=jnp.int32) < live_count
    coefficients = jnp.einsum(
        "fkl,il->fik", u_blocks, vector_row, preferred_element_type=jnp.float32
    ).astype(jnp.bfloat16)
    near_terms = jnp.einsum("im,jml->jil", vector_row, near_row, preferred_element_type=jnp.float32)
    offsets = near_targets - position
    far_after = 0.0
    products = masked_products(coefficients, v_blocks, live_slots)
    places = slot_places(targets, live_slots, capacity, row_count)
    buffer = (
        jnp.zeros((row_count * capacity, rhs_count, width), jnp.float32)
        .at[places]
        .set(products, mode="drop")
    )
    received = lax.all_to_all(buffer, "rows", split_axis=0, concat_axis=0, tiled=True)
    far_sum = jnp.sum(received, axis=0)
    partial_value = far_sum + jnp.sum(
        jnp.where((offsets == 0)[:, None, None], near_terms, 0.0), axis=0
    )
    for direction in (1, -1):
        outgoing = jnp.sum(
            jnp.where((offsets == direction)[:, None, None], near_terms, 0.0), axis=0
        )
        partial_value = partial_value + passed_along(outgoing, "rows", direction)
    result = lax.psum_scatter(partial_value, "blocks", scatter_dimension=0, tiled=True) + far_after
    return result[None]


def solution(mesh):
    in_specs = (
        P(("groups", "rows"), None, None),
        P(("groups", "rows"), "blocks", None, None, None),
        P(("groups", "rows"), "blocks", None, None, None),
        P(("groups", "rows"), "blocks", None),
        P(("groups", "rows"), "blocks"),
        P(("groups", "rows"), "blocks", None, None, None),
        P(("groups", "rows"), "blocks", None),
    )
    out_specs = P(("groups", "rows"), "blocks", None)
    return jax.shard_map(
        on_device, mesh=mesh, in_specs=in_specs, out_specs=out_specs, check_vma=False
    )
```

profile of v0, /device:TPU:0, one launch (start us, length us, event | category | flops | bytes accessed | tf_op | source)
XLA Modules:
  0.0 106.0 jit_solution(2066864060681228767)
XLA Ops:
  6.5 0.0 copy-start
  6.5 0.0 copy-start.3
  7.4 0.8 copy-done
  8.1 3.0 %fusion.2 = bf16[16,128,32]{1,0,2:T(8,128)(2,1)S(1)} fusion(bf16[128,32,256]{2,1,0:T(8,128)(2,1)S(1)} %bitcast.54, bf16[1,16,256]{2,1,0:T(8,128)(2,1)} %param.7), kind=kOutput, calls=%fused_computation.3 | convolution fusion | flops 33554432 | bytes 2236416 | tf_op jit(solution)/shard_map/fkl,il->fik/dot_general | solution.py:46
  11.1 0.5 copy.9
  11.6 0.0 copy-done.3
  11.6 0.2 convert_reduce_fusion
  11.8 3.3 %fusion.4 = f32[128,16,256]{2,1,0:T(8,128)} fusion(bf16[1,1,128,32,256]{4,3,2,1,0:T(8,128)(2,1)} %param.9, pred[128]{0:T(512)(128)(4,1)S(1)} %iota_compare_fusion.1, bf16[16,128,32]{2,0,1:T(8,128)(2,1)S(1)} %copy.9), kind=kOutput, calls=%fused_computation.5 | convolution fusion | flops 34078720 | bytes 4325504 | tf_op jit(solution)/shard_map/fik,fkl->fil/dot_general | solution.py:25
  15.1 1.6 %broadcast_in_dim.52 = f32[128,16,256]{2,1,0:T(8,128)} broadcast(f32[]{:T(128)} %constant.8.clone.1), dimensions={} | broadcast | bytes 2097156 | tf_op jit(solution)/shard_map/broadcast_in_dim | solution.py:55
  16.7 17.2 %scatter_fusion = f32[128,16,256]{2,1,0:T(8,128)} fusion(f32[128,16,256]{2,1,0:T(8,128)} %broadcast_in_dim.52, s32[128]{0:T(128)S(1)} %fusion.16, f32[128,16,256]{2,1,0:T(8,128)} %fusion.4), kind=kCustom, calls=%fused_computation | custom fusion | bytes 6291968 | tf_op jit(solution)/shard_map/scatter | solution.py:57
  34.0 0.0 copy-start.4
  34.0 0.0 copy-start.1
  34.0 0.0 copy-start.2
  34.0 7.3 %all-to-all-start = ((f32[128,16,256]{2,1,0:T(8,128)}), f32[128,16,256]{2,1,0:T(8,128)}, u32[]{:S(2)}, u32[]{:S(2)}) async-start(f32[128,16,256]{2,1,0:T(8,128)} %scatter_fusion), calls=%async_computation | async-start | bytes 4194304 | tf_op jit(solution)/shard_map/all_to_all | solution.py:59
  41.3 0.0 reduce-scatter.2.cloned.1.call-start
  41.4 0.0 copy-done.4
  41.4 0.0 copy-done.1
  41.4 0.0 copy-done.2
  41.4 0.2 select_reduce_fusion.2
  41.6 1.3 %collective-permute-start.1 = (f32[16,256]{1,0:T(8,128)S(1)}, f32[16,256]{1,0:T(8,128)S(1)}, u32[]{:S(2)}, u32[]{:S(2)}) collective-permute-start(f32[16,256]{1,0:T(8,128)S(1)} %bitcast.56), channel_id=1, source_target_pairs={{2,0},{4,2},{6,4},{8,6},{10,8},{12,10},{14,12},{3,1},{5,3},{7,5},{... | collective-permute-start | bytes 49160 | tf_op jit(solution)/shard_map/ppermute | solution.py:10
  42.9 4.5 %collective-permute-start = (f32[16,256]{1,0:T(8,128)S(1)}, f32[16,256]{1,0:T(8,128)S(1)}, u32[]{:S(2)}, u32[]{:S(2)}) collective-permute-start(f32[16,256]{1,0:T(8,128)S(1)} %bitcast.55), channel_id=1, source_target_pairs={{0,2},{2,4},{4,6},{6,8},{8,10},{10,12},{12,14},{1,3},{3,5},{5,7},{... | collective-permute-start | bytes 49160 | tf_op jit(solution)/shard_map/ppermute | solution.py:10
  47.5 42.4 %all-to-all-done = f32[128,16,256]{2,1,0:T(8,128)} async-done(((f32[128,16,256]{2,1,0:T(8,128)}), f32[128,16,256]{2,1,0:T(8,128)}, u32[]{:S(2)}, u32[]{:S(2)}) %all-to-all-start) | async-done | bytes 2097184 | tf_op jit(solution)/shard_map/all_to_all | solution.py:59
  89.8 1.8 %reduce_sum.55 = f32[16,256]{1,0:T(8,128)S(1)} reduce(f32[128,16,256]{2,1,0:T(8,128)} %all-to-all-done, f32[]{:T(128)} %constant.8.clone.1), dimensions={0}, to_apply=%region_2.3 | reduce | flops 520192 | bytes 2113540 | tf_op jit(solution)/shard_map/reduce_sum | solution.py:60
  91.6 0.0 collective-permute-done.1
  91.6 0.0 collective-permute-done
  91.6 0.6 fusion.13
  92.2 0.0 reduce-scatter.2.cloned.1.call-update
  92.3 6.9 %reduce-scatter.2.cloned.1.call-done = f32[8,256]{1,0:T(8,128)} async-done(((f32[16,256]{1,0:T(8,128)}), f32[8,256]{1,0:T(8,128)}) %reduce-scatter.2.cloned.1.call-update) | async-done | bytes 8208 | tf_op jit(solution)/shard_map/reduce_scatter | solution.py:69
  (3 shorter events, 0.0 us)
Async XLA Ops:
  6.5 1.6 %copy-start = (bf16[1,1,128,32,256]{4,3,2,1,0:T(8,128)(2,1)S(1)}, bf16[1,1,128,32,256]{4,3,2,1,0:T(8,128)(2,1)}, u32[]{:S(2)}) copy-start(bf16[1,1,128,32,256]{4,3,2,1,0:T(8,128)(2,1)} %param.8) | copy-start | bytes 6291460
  6.5 5.1 %copy-start.3 = (s32[1,1,128]{2,1,0:T(1,128)S(1)}, s32[1,1,128]{2,1,0:T(1,128)}, u32[]{:S(2)}) copy-start(s32[1,1,128]{2,1,0:T(1,128)} %param.10) | copy-start | bytes 1540
  34.0 7.4 %copy-start.4 = (s32[1,1,4]{2,1,0:T(1,128)S(1)}, s32[1,1,4]{2,1,0:T(1,128)}, u32[]{:S(2)}) copy-start(s32[1,1,4]{2,1,0:T(1,128)} %param.13) | copy-start | bytes 52
  34.0 7.4 %copy-start.1 = (bf16[1,1,4,256,256]{4,3,2,1,0:T(8,128)(2,1)S(1)}, bf16[1,1,4,256,256]{4,3,2,1,0:T(8,128)(2,1)}, u32[]{:S(2)}) copy-start(bf16[1,1,4,256,256]{4,3,2,1,0:T(8,128)(2,1)} %param.12) | copy-start | bytes 1572868
  34.0 7.4 %copy-start.2 = (bf16[1,16,256]{2,1,0:T(8,128)(2,1)S(1)}, bf16[1,16,256]{2,1,0:T(8,128)(2,1)}, u32[]{:S(2)}) copy-start(bf16[1,16,256]{2,1,0:T(8,128)(2,1)} %param.7) | copy-start | bytes 24580
  34.0 55.9 %all-to-all-start = ((f32[128,16,256]{2,1,0:T(8,128)}), f32[128,16,256]{2,1,0:T(8,128)}, u32[]{:S(2)}, u32[]{:S(2)}) async-start(f32[128,16,256]{2,1,0:T(8,128)} %scatter_fusion), calls=%async_computation | async-start | bytes 4194304 | tf_op jit(solution)/shard_map/all_to_all | solution.py:59
  41.3 57.9 %reduce-scatter.2.cloned.1.call-start = ((), (), s32[]{:S(2)}) async-start(), calls=%async_computation.2 | async-start | bytes 24576 | tf_op jit(solution)/shard_map/reduce_scatter | solution.py:69
  41.6 50.0 %collective-permute-start.1 = (f32[16,256]{1,0:T(8,128)S(1)}, f32[16,256]{1,0:T(8,128)S(1)}, u32[]{:S(2)}, u32[]{:S(2)}) collective-permute-start(f32[16,256]{1,0:T(8,128)S(1)} %bitcast.56), channel_id=1, source_target_pairs={{2,0},{4,2},{6,4},{8,6},{10,8},{12,10},{14,12},{3,1},{5,3},{7,5},{... | collective-permute-start | bytes 49160 | tf_op jit(solution)/shard_map/ppermute | solution.py:10
  42.9 48.7 %collective-permute-start = (f32[16,256]{1,0:T(8,128)S(1)}, f32[16,256]{1,0:T(8,128)S(1)}, u32[]{:S(2)}, u32[]{:S(2)}) collective-permute-start(f32[16,256]{1,0:T(8,128)S(1)} %bitcast.55), channel_id=1, source_target_pairs={{0,2},{2,4},{4,6},{6,8},{8,10},{10,12},{12,14},{1,3},{3,5},{5,7},{... | collective-permute-start | bytes 49160 | tf_op jit(solution)/shard_map/ppermute | solution.py:10
Sparse Core Ops, SparseCore 0:
  92.4 6.7 reduce-scatter.1
where the time goes:
time: 107 us; the launch traced here: 106 us
  waiting for transfers between devices  49.3 us (46%)
  local copies, waits for them, and re-layouts  20.1 us (19%)
  between operations  14.3 us (13%)
  starting transfers between devices  13.2 us (12%)
  matrix products  6.49 us (6%)
  other arithmetic  2.57 us (2%)
    all_to_all x1, waiting for transfers between devices, on_device(): lax.all_to_all(buffer, 'rows', split_axis=0, concat_axis=0, tiled=True)  42.4 us
    scatter x1, local copies, waits for them, and re-layouts, on_device(): buffer = jnp.zeros((row_count * capacity, rhs_count, width), jnp.float32)...  17.2 us
    all_to_all x1, starting transfers between devices, on_device(): lax.all_to_all(buffer, 'rows', split_axis=0, concat_axis=0, tiled=True)  7.34 us
    reduce_scatter x1, waiting for transfers between devices, on_device(): lax.psum_scatter(partial_value, 'blocks', scatter_dimension=0, tiled=True)  6.93 us
    ppermute x2, starting transfers between devices, passed_along(): return lax.ppermute(x, axis, pairs)  5.84 us
    dot_general x1, matrix products, masked_products(): jnp.einsum('fik,fkl->fil', coefficients, v_blocks, preferred_element_type...  3.31 us
    dot_general x1, matrix products, on_device(): jnp.einsum('fkl,il->fik', u_blocks, vector_row, preferred_element_type=jn...  3 us
  transfers between devices with their start and end apart: 4, of which 2 were waited for; matrix products, arithmetic and copies ran while one was open for 2% of the time, Pallas kernels for 0%

commit v1 on v0

v1 whole, which is shorter than its diff:
```python
import functools
import math

import jax
import jax.numpy as jnp
from jax import lax
from jax.experimental import pallas as pl
from jax.experimental.pallas import tpu as pltpu
from jax.sharding import PartitionSpec as P

LANES = 128
CHUNKS = 4
UNROLLED = 16


def each(count, step):
    if count <= UNROLLED:
        for index in range(count):
            step(index)
    else:
        pl.loop(0, count)(step)


def product_kernel(
    row_count, block_count,
    vector_hbm, u_hbm, v_hbm, cols_hbm, counts_hbm, near_hbm, near_cols_hbm,
    out_ref,
    vector, u, v, near, cols, counts, near_cols, coefficients, partial,
    outgoing, incoming, load_sems, chunk_sems, send_sem, recv_sem,
):
    far_total, rank, width = u.shape
    near_total = near.shape[0]
    rhs_count = vector.shape[0]
    half = rhs_count // block_count
    pieces = width // LANES
    device_total = row_count * block_count
    me = lax.axis_index("rows") * block_count + lax.axis_index("blocks")
    chunk = far_total // CHUNKS
    depth = chunk * rank
    group = math.gcd(row_count, 8)

    def loaded(hbm, here, sem):
        copy = pltpu.make_async_copy(hbm, here, load_sems.at[sem])
        copy.start()
        return copy

    def chunk_loaded(hbm, here, part, which):
        slots = pl.ds(part * chunk, chunk)
        copy = pltpu.make_async_copy(
            hbm.at[0, 0, slots], here.at[slots], chunk_sems.at[which, part]
        )
        copy.start()
        return copy

    vector_copy = loaded(vector_hbm.at[0], vector, 0)
    cols_copy = loaded(cols_hbm, cols, 1)
    counts_copy = loaded(counts_hbm, counts, 2)
    near_cols_copy = loaded(near_cols_hbm, near_cols, 3)
    u_copies = [chunk_loaded(u_hbm, u, part, 0) for part in range(CHUNKS)]
    near_copy = loaded(near_hbm.at[0, 0], near, 4)
    v_copies = [chunk_loaded(v_hbm, v, part, 1) for part in range(CHUNKS)]

    def partner(distance):
        other = lax.rem(me + distance, device_total)
        return {"rows": other // block_count, "blocks": lax.rem(other, block_count)}

    barrier = pltpu.get_barrier_semaphore()

    def greet(index):
        pl.semaphore_signal(
            barrier, inc=1, device_id=partner(index + 1), device_id_type=pl.DeviceIdType.MESH
        )

    each(device_total - 1, greet)

    cols_copy.wait()
    counts_copy.wait()
    near_cols_copy.wait()
    live_count = counts[0, 0]
    vector_copy.wait()
    vector_row = vector[...]

    def slot_cols(part):
        lanes = lax.broadcasted_iota(jnp.int32, (rhs_count, LANES), 1)
        across = LANES // rank
        tiles = []
        for tile in range(depth // LANES):
            first = part * chunk + tile * across
            tile_cols = jnp.full((rhs_count, LANES), cols[0, 0, first], jnp.int32)
            for place in range(1, across):
                tile_cols = jnp.where(lanes >= place * rank, cols[0, 0, first + place], tile_cols)
            tiles.append(jnp.where(first + lanes // rank < live_count, tile_cols, -1))
        return jnp.concatenate(tiles, axis=1)

    def far_rows(part, first_cluster, chunk_coefficients):
        chunk_cols = slot_cols(part)
        rows = [
            jnp.where(chunk_cols == first_cluster + index, chunk_coefficients, 0.0)
            for index in range(group)
        ]
        return jnp.concatenate(rows, axis=0).astype(jnp.bfloat16)

    def chunk_coefficients(part):
        blocks = u[part * chunk:(part + 1) * chunk].reshape(depth, width)
        return lax.dot_general(
            vector_row, blocks, (((1,), (1,)), ((), ())), preferred_element_type=jnp.float32
        )

    def v_blocks(part):
        return v[part * chunk:(part + 1) * chunk].reshape(depth, width)

    def near_term(index):
        return jnp.dot(vector_row, near[index], preferred_element_type=jnp.float32)

    def near_sum(first_cluster, terms):
        rows = []
        for index in range(group):
            row = jnp.zeros((rhs_count, width), jnp.float32)
            for place in range(near_total):
                named = (near_cols[0, 0, place] == first_cluster + index).astype(jnp.float32)
                row = row + named * terms[place]
            rows.append(row)
        return jnp.concatenate(rows, axis=0)

    def put(first_cluster, total):
        first_row = first_cluster * rhs_count
        if not isinstance(first_row, int):
            first_row = pl.multiple_of(first_row, group * rhs_count)
        partial[pl.ds(first_row, group * rhs_count)] = total
        for index in range(group * block_count):
            rows = total[index * half:(index + 1) * half]
            outgoing[first_cluster * block_count + index] = jnp.concatenate(
                [rows[:, piece * LANES:(piece + 1) * LANES] for piece in range(pieces)], axis=0
            ).astype(jnp.bfloat16)

    if row_count == group:
        far = []
        for part in range(CHUNKS):
            u_copies[part].wait()
            far.append(far_rows(part, 0, chunk_coefficients(part)))
        near_copy.wait()
        total = near_sum(0, [near_term(index) for index in range(near_total)])
        for part in range(CHUNKS):
            v_copies[part].wait()
            total = total + jnp.dot(far[part], v_blocks(part), preferred_element_type=jnp.float32)
        put(0, total)
    else:
        for part in range(CHUNKS):
            u_copies[part].wait()
            coefficients[:, part * depth:(part + 1) * depth] = chunk_coefficients(part)
        near_copy.wait()
        for part in range(CHUNKS):
            v_copies[part].wait()

        @pl.loop(0, row_count // group)
        def _(step):
            first_cluster = step * group
            total = near_sum(first_cluster, [near_term(index) for index in range(near_total)])
            for part in range(CHUNKS):
                held = coefficients[:, part * depth:(part + 1) * depth]
                total = total + jnp.dot(
                    far_rows(part, first_cluster, held), v_blocks(part),
                    preferred_element_type=jnp.float32,
                )
            put(first_cluster, total)

    pl.semaphore_wait(barrier, device_total - 1)

    def send(index):
        distance = index + 1
        pltpu.make_async_remote_copy(
            src_ref=outgoing.at[lax.rem(me + distance, device_total)],
            dst_ref=incoming.at[index],
            send_sem=send_sem,
            recv_sem=recv_sem,
            device_id=partner(distance),
            device_id_type=pl.DeviceIdType.MESH,
        ).start()

    each(device_total - 1, send)

    own = partial[pl.ds(pl.multiple_of(me * half, half), half)]
    pltpu.make_async_copy(incoming, incoming, recv_sem).wait()
    arrived = jnp.sum(incoming[...].astype(jnp.float32), axis=0)
    out_ref[0] = own + jnp.concatenate(
        [arrived[piece * half:(piece + 1) * half] for piece in range(pieces)], axis=1
    )
    pltpu.make_async_copy(incoming, incoming, send_sem).wait()


def on_device(row_count, block_count, adjoint_in, far_u, far_v, far_cols, far_counts, near_blocks, near_cols):
    far_total, rank, width = far_u.shape[2:]
    rhs_count = adjoint_in.shape[1]
    half = rhs_count // block_count
    device_total = row_count * block_count
    message = (half * width // LANES, LANES)
    in_place = pl.BlockSpec(memory_space=pl.ANY)
    return pl.pallas_call(
        functools.partial(product_kernel, row_count, block_count),
        out_shape=jax.ShapeDtypeStruct((1, half, width), jnp.float32),
        in_specs=[in_place] * 7,
        out_specs=pl.BlockSpec(memory_space=pltpu.VMEM),
        scratch_shapes=[
            pltpu.VMEM((rhs_count, width), jnp.bfloat16),
            pltpu.VMEM((far_total, rank, width), jnp.bfloat16),
            pltpu.VMEM((far_total, rank, width), jnp.bfloat16),
            pltpu.VMEM(near_blocks.shape[2:], jnp.bfloat16),
            pltpu.SMEM(far_cols.shape, jnp.int32),
            pltpu.SMEM(far_counts.shape, jnp.int32),
            pltpu.SMEM(near_cols.shape, jnp.int32),
            pltpu.VMEM((rhs_count, far_total * rank), jnp.float32),
            pltpu.VMEM((row_count * rhs_count, width), jnp.float32),
            pltpu.VMEM((device_total,) + message, jnp.bfloat16),
            pltpu.VMEM((device_total - 1,) + message, jnp.bfloat16),
            pltpu.SemaphoreType.DMA((5,)),
            pltpu.SemaphoreType.DMA((2, CHUNKS)),
            pltpu.SemaphoreType.DMA,
            pltpu.SemaphoreType.DMA,
        ],
        compiler_params=pltpu.CompilerParams(
            collective_id=0, has_side_effects=True, vmem_limit_bytes=63 * 1024 * 1024
        ),
    )(adjoint_in, far_u, far_v, far_cols, far_counts, near_blocks, near_cols)


def solution(mesh):
    in_specs = (
        P(("groups", "rows"), None, None),
        P(("groups", "rows"), "blocks", None, None, None),
        P(("groups", "rows"), "blocks", None, None, None),
        P(("groups", "rows"), "blocks", None),
        P(("groups", "rows"), "blocks"),
        P(("groups", "rows"), "blocks", None, None, None),
        P(("groups", "rows"), "blocks", None),
    )
    out_specs = P(("groups", "rows"), "blocks", None)
    return jax.shard_map(
        functools.partial(on_device, mesh.shape["rows"], mesh.shape["blocks"]),
        mesh=mesh, in_specs=in_specs, out_specs=out_specs, check_vma=False,
    )
```

time: 107 us -> 14 us (0.13)
  waiting for transfers between devices: 49.3 us -> 0 us
  local copies, waits for them, and re-layouts: 20.1 us -> 1.3 us
  between operations: 14.3 us -> 0.66 us
  starting transfers between devices: 13.2 us -> 0 us
  Pallas kernels: 0 us -> 11.8 us
  matrix products: 6.49 us -> 0 us
  other arithmetic: 2.57 us -> 0 us
    all_to_all x1 -> x0, waiting for transfers between devices: 42.4 us -> none  [on_device(): lax.all_to_all(buffer, 'rows', split_axis=0, concat_axis=0, tiled=True)]
    scatter x1 -> x0, local copies, waits for them, and re-layouts: 17.2 us -> none  [on_device(): buffer = jnp.zeros((row_count * capacity, rhs_count, width), jnp.float32)...]
    pallas_call x0 -> x1, Pallas kernels: none -> 11.8 us  [on_device(): pl.pallas_call(functools.partial(product_kernel, row_count, block_count),...]
    all_to_all x1 -> x0, starting transfers between devices: 7.34 us -> none  [on_device(): lax.all_to_all(buffer, 'rows', split_axis=0, concat_axis=0, tiled=True)]
    reduce_scatter x1 -> x0, waiting for transfers between devices: 6.93 us -> none  [on_device(): lax.psum_scatter(partial_value, 'blocks', scatter_dimension=0, tiled=True)]
    dot_general x3 -> x0, matrix products: 6.49 us -> none  [the longest x1 3.31 us: masked_products(): jnp.einsum('fik,fkl->fil', coefficients, v_blocks, preferred_element_type...]
    ppermute x2 -> x0, starting transfers between devices: 5.84 us -> none  [passed_along(): return lax.ppermute(x, axis, pairs)]
    reduce_sum x2 -> x0, other arithmetic: 1.95 us -> none  [the longest x1 1.78 us: on_device(): far_sum = jnp.sum(received, axis=0)]
  transfers between devices with their start and end apart: 4 -> 0, of which waited for: 2 -> 0; matrix products, arithmetic and copies ran while one was open for 2% -> 0% of each run, Pallas kernels for 0% -> 0%
where the time goes in v1:
time: 14 us; the launch traced here: 13.8 us
  Pallas kernels  11.8 us (84%)
  local copies, waits for them, and re-layouts  1.3 us (9%)
  between operations  0.66 us (5%)
    pallas_call x1, Pallas kernels, on_device(): pl.pallas_call(functools.partial(product_kernel, row_count, block_count),...  11.8 us
    unnamed x1, local copies, waits for them, and re-layouts  1.3 us

profile of v1, /device:TPU:0, one launch (start us, length us, event | category | flops | bytes accessed | tf_op | source)
XLA Modules:
  0.0 13.8 jit_solution(9367701849813876235)
XLA Ops:
  0.7 11.8 %shard_map.73 = f32[1,8,256]{2,1,0:T(8,128)} custom-call(bf16[1,16,256]{2,1,0:T(8,128)(2,1)} %vector_hbm.1, bf16[1,1,128,32,256]{4,3,2,1,0:T(8,128)(2,1)} %u_hbm.1, bf16[1,1,128,32,256]{4,3,2,1,0:T(8,128)(2,1)} %v_hbm.1, s32[1,1,128]{2,1,0:T(1,128)} %cols_hbm.1, s32[1,1]{1,0:T(1,128)S(6)} %copy.9.counts_hbm, bf16[1,1,4,256,256]{4,3,2,1,0:T(8,128)(2,1)} %near_hbm.1, ...), custom_call_target="tpu_custom_call" | custom-call | tf_op jit(solution)/shard_map/pallas_call | solution.py:198
  12.5 1.3 %copy.10 = f32[1,8,256]{2,1,0:T(8,128)} copy(f32[1,8,256]{2,1,0:T(8,128)} %shard_map.73) | data formatting | bytes 16384

commit v2 on v1

--- a/solution.py
+++ b/solution.py
@@ -9,7 +9,7 @@
 from jax.sharding import PartitionSpec as P
 
 LANES = 128
-CHUNKS = 4
+CHUNKS = 1
 UNROLLED = 16
 
 
@@ -25,14 +25,12 @@
     row_count, block_count,
     vector_hbm, u_hbm, v_hbm, cols_hbm, counts_hbm, near_hbm, near_cols_hbm,
     out_ref,
-    vector, u, v, near, cols, counts, near_cols, coefficients, partial,
-    outgoing, incoming, load_sems, chunk_sems, send_sem, recv_sem,
+    vector, u, v, near, cols, counts, near_cols, masks, partial, load_sems, chunk_sems, send_sem, recv_sem,
 ):
     far_total, rank, width = u.shape
     near_total = near.shape[0]
     rhs_count = vector.shape[0]
     half = rhs_count // block_count
-    pieces = width // LANES
     device_total = row_count * block_count
     me = lax.axis_index("rows") * block_count + lax.axis_index("blocks")
     chunk = far_total // CHUNKS
@@ -60,9 +58,14 @@
     near_copy = loaded(near_hbm.at[0, 0], near, 4)
     v_copies = [chunk_loaded(v_hbm, v, part, 1) for part in range(CHUNKS)]
 
+    row = lax.axis_index("rows")
+    block = lax.axis_index("blocks")
+
     def partner(distance):
-        other = lax.rem(me + distance, device_total)
-        return {"rows": other // block_count, "blocks": lax.rem(other, block_count)}
+        return {
+            "rows": lax.rem(row + distance // block_count, row_count),
+            "blocks": lax.rem(block + distance % block_count, block_count),
+        }
 
     barrier = pltpu.get_barrier_semaphore()
 
@@ -92,19 +95,25 @@
             tiles.append(jnp.where(first + lanes // rank < live_count, tile_cols, -1))
         return jnp.concatenate(tiles, axis=1)
 
-    def far_rows(part, first_cluster, chunk_coefficients):
-        chunk_cols = slot_cols(part)
-        rows = [
-            jnp.where(chunk_cols == first_cluster + index, chunk_coefficients, 0.0)
-            for index in range(group)
-        ]
-        return jnp.concatenate(rows, axis=0).astype(jnp.bfloat16)
+    def put_masks(first_cluster):
+        for part in range(CHUNKS):
+            part_cols = slot_cols(part)
+            for index in range(group):
+                masks[index, :, part * depth:(part + 1) * depth] = jnp.where(
+                    part_cols == first_cluster + index, 1.0, 0.0
+                ).astype(jnp.bfloat16)
+
+    def far_rows(part, coefficients):
+        return jnp.concatenate(
+            [coefficients * masks[index, :, part * depth:(part + 1) * depth] for index in range(group)],
+            axis=0,
+        )
 
     def chunk_coefficients(part):
         blocks = u[part * chunk:(part + 1) * chunk].reshape(depth, width)
         return lax.dot_general(
             vector_row, blocks, (((1,), (1,)), ((), ())), preferred_element_type=jnp.float32
-        )
+        ).astype(jnp.bfloat16)
 
     def v_blocks(part):
         return v[part * chunk:(part + 1) * chunk].reshape(depth, width)
@@ -127,65 +136,63 @@
         if not isinstance(first_row, int):
             first_row = pl.multiple_of(first_row, group * rhs_count)
         partial[pl.ds(first_row, group * rhs_count)] = total
-        for index in range(group * block_count):
-            rows = total[index * half:(index + 1) * half]
-            outgoing[first_cluster * block_count + index] = jnp.concatenate(
-                [rows[:, piece * LANES:(piece + 1) * LANES] for piece in range(pieces)], axis=0
-            ).astype(jnp.bfloat16)
 
     if row_count == group:
+        put_masks(0)
         far = []
         for part in range(CHUNKS):
             u_copies[part].wait()
-            far.append(far_rows(part, 0, chunk_coefficients(part)))
+            far.append(far_rows(part, chunk_coefficients(part)))
         near_copy.wait()
         total = near_sum(0, [near_term(index) for index in range(near_total)])
         for part in range(CHUNKS):
             v_copies[part].wait()
-            total = total + jnp.dot(far[part], v_blocks(part), preferred_element_type=jnp.float32)
+            total = total + jnp.concatenate([
+                jnp.dot(far[part], v_blocks(part)[:, piece:piece + LANES], preferred_element_type=jnp.float32)
+                for piece in range(0, width, LANES)
+            ], axis=1)
         put(0, total)
     else:
+        near_copy.wait()
         for part in range(CHUNKS):
             u_copies[part].wait()
-            coefficients[:, part * depth:(part + 1) * depth] = chunk_coefficients(part)
-        near_copy.wait()
-        for part in range(CHUNKS):
             v_copies[part].wait()
 
         @pl.loop(0, row_count // group)
         def _(step):
             first_cluster = step * group
+            put_masks(first_cluster)
             total = near_sum(first_cluster, [near_term(index) for index in range(near_total)])
             for part in range(CHUNKS):
-                held = coefficients[:, part * depth:(part + 1) * depth]
                 total = total + jnp.dot(
-                    far_rows(part, first_cluster, held), v_blocks(part),
+                    far_rows(part, chunk_coefficients(part)), v_blocks(part),
                     preferred_element_type=jnp.float32,
                 )
             put(first_cluster, total)
 
     pl.semaphore_wait(barrier, device_total - 1)
 
+    def rows_of(device):
+        return partial.at[pl.ds(pl.multiple_of(device * half, half), half)]
+
     def send(index):
-        distance = index + 1
+        other = partner(index + 1)
         pltpu.make_async_remote_copy(
-            src_ref=outgoing.at[lax.rem(me + distance, device_total)],
-            dst_ref=incoming.at[index],
+            src_ref=rows_of(other["rows"] * block_count + other["blocks"]),
+            dst_ref=out_ref.at[index],
             send_sem=send_sem,
             recv_sem=recv_sem,
-            device_id=partner(distance),
+            device_id=other,
             device_id_type=pl.DeviceIdType.MESH,
         ).start()
 
     each(device_total - 1, send)
 
-    own = partial[pl.ds(pl.multiple_of(me * half, half), half)]
-    pltpu.make_async_copy(incoming, incoming, recv_sem).wait()
-    arrived = jnp.sum(incoming[...].astype(jnp.float32), axis=0)
-    out_ref[0] = own + jnp.concatenate(
-        [arrived[piece * half:(piece + 1) * half] for piece in range(pieces)], axis=1
-    )
-    pltpu.make_async_copy(incoming, incoming, send_sem).wait()
+    own_copy = loaded(rows_of(me), out_ref.at[device_total - 1], 0)
+    arrivals = out_ref.at[pl.ds(0, device_total - 1)]
+    pltpu.make_async_copy(arrivals, arrivals, recv_sem).wait()
+    pltpu.make_async_copy(arrivals, arrivals, send_sem).wait()
+    own_copy.wait()
 
 
 def on_device(row_count, block_count, adjoint_in, far_u, far_v, far_cols, far_counts, near_blocks, near_cols):
@@ -193,13 +200,12 @@
     rhs_count = adjoint_in.shape[1]
     half = rhs_count // block_count
     device_total = row_count * block_count
-    message = (half * width // LANES, LANES)
     in_place = pl.BlockSpec(memory_space=pl.ANY)
-    return pl.pallas_call(
+    received = pl.pallas_call(
         functools.partial(product_kernel, row_count, block_count),
-        out_shape=jax.ShapeDtypeStruct((1, half, width), jnp.float32),
+        out_shape=jax.ShapeDtypeStruct((device_total, half, width), jnp.float32),
         in_specs=[in_place] * 7,
-        out_specs=pl.BlockSpec(memory_space=pltpu.VMEM),
+        out_specs=in_place,
         scratch_shapes=[
             pltpu.VMEM((rhs_count, width), jnp.bfloat16),
             pltpu.VMEM((far_total, rank, width), jnp.bfloat16),
@@ -208,10 +214,8 @@
             pltpu.SMEM(far_cols.shape, jnp.int32),
             pltpu.SMEM(far_counts.shape, jnp.int32),
             pltpu.SMEM(near_cols.shape, jnp.int32),
-            pltpu.VMEM((rhs_count, far_total * rank), jnp.float32),
+            pltpu.VMEM((math.gcd(row_count, 8), rhs_count, far_total * rank), jnp.bfloat16),
             pltpu.VMEM((row_count * rhs_count, width), jnp.float32),
-            pltpu.VMEM((device_total,) + message, jnp.bfloat16),
-            pltpu.VMEM((device_total - 1,) + message, jnp.bfloat16),
             pltpu.SemaphoreType.DMA((5,)),
             pltpu.SemaphoreType.DMA((2, CHUNKS)),
             pltpu.SemaphoreType.DMA,
@@ -221,6 +225,7 @@
             collective_id=0, has_side_effects=True, vmem_limit_bytes=63 * 1024 * 1024
         ),
     )(adjoint_in, far_u, far_v, far_cols, far_counts, near_blocks, near_cols)
+    return jnp.sum(received, axis=0, keepdims=True)
 
 
 def solution(mesh):

time: 14 us -> 13.4 us (0.957)
  other arithmetic: 0 us -> 1.52 us
  local copies, waits for them, and re-layouts: 1.3 us -> 0 us
  Pallas kernels: 11.8 us -> 11.1 us
    reduce_sum x0 -> x1, other arithmetic: none -> 1.52 us  [on_device(): return jnp.sum(received, axis=0, keepdims=True)]
    unnamed x1 -> x0, local copies, waits for them, and re-layouts: 1.3 us -> none
    pallas_call x1, Pallas kernels: 11.8 us -> 11.1 us  [on_device(): pl.pallas_call(functools.partial(product_kernel, row_count, block_count),...]
where the time goes in v2:
time: 13.4 us; the launch traced here: 13.3 us
  Pallas kernels  11.1 us (83%)
  other arithmetic  1.52 us (11%)
  between operations  0.66 us (5%)
    pallas_call x1, Pallas kernels, on_device(): pl.pallas_call(functools.partial(product_kernel, row_count, block_count),...  11.1 us
    reduce_sum x1, other arithmetic, on_device(): return jnp.sum(received, axis=0, keepdims=True)  1.52 us

profile of v2, /device:TPU:0, one launch (start us, length us, event | category | flops | bytes accessed | tf_op | source)
XLA Modules:
  0.0 13.3 jit_solution(4877232883030888346)
XLA Ops:
  0.7 11.1 %shard_map.73 = f32[16,8,256]{2,1,0:T(8,128)} custom-call(bf16[1,16,256]{2,1,0:T(8,128)(2,1)} %vector_hbm.1, bf16[1,1,128,32,256]{4,3,2,1,0:T(8,128)(2,1)} %u_hbm.1, bf16[1,1,128,32,256]{4,3,2,1,0:T(8,128)(2,1)} %v_hbm.1, s32[1,1,128]{2,1,0:T(1,128)} %cols_hbm.1, s32[1,1]{1,0:T(1,128)S(6)} %copy.8.counts_hbm, bf16[1,1,4,256,256]{4,3,2,1,0:T(8,128)(2,1)} %near_hbm.1, ...), custom_call_target="tpu_custom_call" | custom-call | tf_op jit(solution)/shard_map/pallas_call | solution.py:204
  11.7 1.5 %reduce_sum.9 = f32[8,256]{1,0:T(8,128)} reduce(f32[16,8,256]{2,1,0:T(8,128)} %shard_map.73, f32[]{:T(128)} %constant.0.clone.1), dimensions={0}, to_apply=%region_0.0 | reduce | flops 30720 | bytes 139268 | tf_op jit(solution)/shard_map/reduce_sum | solution.py:228

commit v3 on v2

--- a/solution.py
+++ b/solution.py
@@ -9,7 +9,7 @@
 from jax.sharding import PartitionSpec as P
 
 LANES = 128
-CHUNKS = 1
+CHUNKS = 2
 UNROLLED = 16
 
 
@@ -25,7 +25,7 @@
     row_count, block_count,
     vector_hbm, u_hbm, v_hbm, cols_hbm, counts_hbm, near_hbm, near_cols_hbm,
     out_ref,
-    vector, u, v, near, cols, counts, near_cols, masks, partial, load_sems, chunk_sems, send_sem, recv_sem,
+    vector, u, v, near, cols, counts, near_cols, masks, far, partial, load_sems, chunk_sems, send_sem, recv_sem,
 ):
     far_total, rank, width = u.shape
     near_total = near.shape[0]
@@ -139,16 +139,18 @@
 
     if row_count == group:
         put_masks(0)
-        far = []
         for part in range(CHUNKS):
             u_copies[part].wait()
-            far.append(far_rows(part, chunk_coefficients(part)))
+            far[:, part * depth:(part + 1) * depth] = far_rows(part, chunk_coefficients(part))
         near_copy.wait()
         total = near_sum(0, [near_term(index) for index in range(near_total)])
         for part in range(CHUNKS):
             v_copies[part].wait()
             total = total + jnp.concatenate([
-                jnp.dot(far[part], v_blocks(part)[:, piece:piece + LANES], preferred_element_type=jnp.float32)
+                jnp.dot(
+                    far[:, part * depth:(part + 1) * depth], v_blocks(part)[:, piece:piece + LANES],
+                    preferred_element_type=jnp.float32,
+                )
                 for piece in range(0, width, LANES)
             ], axis=1)
         put(0, total)
@@ -215,6 +217,7 @@
             pltpu.SMEM(far_counts.shape, jnp.int32),
             pltpu.SMEM(near_cols.shape, jnp.int32),
             pltpu.VMEM((math.gcd(row_count, 8), rhs_count, far_total * rank), jnp.bfloat16),
+            pltpu.VMEM((math.gcd(row_count, 8) * rhs_count, far_total * rank), jnp.bfloat16),
             pltpu.VMEM((row_count * rhs_count, width), jnp.float32),
             pltpu.SemaphoreType.DMA((5,)),
             pltpu.SemaphoreType.DMA((2, CHUNKS)),

time: 13.4 us -> 13.3 us (level)
  no operation moved by 1% of the time
where the time goes in v3:
time: 13.3 us; the launch traced here: 13.2 us
  Pallas kernels  11 us (83%)
  other arithmetic  1.52 us (11%)
  between operations  0.66 us (5%)
    pallas_call x1, Pallas kernels, on_device(): pl.pallas_call(functools.partial(product_kernel, row_count, block_count),...  11 us
    reduce_sum x1, other arithmetic, on_device(): return jnp.sum(received, axis=0, keepdims=True)  1.52 us

profile of v3, /device:TPU:0, one launch (start us, length us, event | category | flops | bytes accessed | tf_op | source)
XLA Modules:
  0.0 13.2 jit_solution(11033289406866304687)
XLA Ops:
  0.7 11.0 %shard_map.73 = f32[16,8,256]{2,1,0:T(8,128)} custom-call(bf16[1,16,256]{2,1,0:T(8,128)(2,1)} %vector_hbm.1, bf16[1,1,128,32,256]{4,3,2,1,0:T(8,128)(2,1)} %u_hbm.1, bf16[1,1,128,32,256]{4,3,2,1,0:T(8,128)(2,1)} %v_hbm.1, s32[1,1,128]{2,1,0:T(1,128)} %cols_hbm.1, s32[1,1]{1,0:T(1,128)S(6)} %copy.8.counts_hbm, bf16[1,1,4,256,256]{4,3,2,1,0:T(8,128)(2,1)} %near_hbm.1, ...), custom_call_target="tpu_custom_call" | custom-call | tf_op jit(solution)/shard_map/pallas_call | solution.py:206
  11.7 1.5 %reduce_sum.9 = f32[8,256]{1,0:T(8,128)} reduce(f32[16,8,256]{2,1,0:T(8,128)} %shard_map.73, f32[]{:T(128)} %constant.0.clone.1), dimensions={0}, to_apply=%region_0.0 | reduce | flops 30720 | bytes 139268 | tf_op jit(solution)/shard_map/reduce_sum | solution.py:231
